TPU v7x, 512 devices: a whole 4x8x8 slice. The times are simulated.
512 devices in a mesh: row: 16 (over z, core), col: 32 (over x, y).
Axes of the slice: x: 4, y: 8, z: 8, core: 2. Of those that a mesh axis runs over, the one named last changes fastest.
Arguments:
- tokens: bfloat16 [256, 16384], P('col', 'row'), may hold values from -6 to 6
- cotangent: bfloat16 [256, 28672], P('row', 'col'), may hold values from -6 to 6
- weights: bfloat16 [2, 16384, 28672], P(None, 'row', 'col'), may hold values from -0.046875 to 0.046875
- adapter_down_master: float32 [2, 16384, 16], P(None, ('row', 'col')), may hold values from -0.046875 to 0.046875
- adapter_up_master: float32 [2, 16, 28672], P(None, None, ('col', 'row')), may hold values from -0.3 to 0.3
- down_first_moment: float32 [2, 16384, 16], P(None, ('row', 'col')), may hold values from -18 to 18
- down_second_moment: float32 [2, 16384, 16], P(None, ('row', 'col')), may hold values from 100 to 3000
- up_first_moment: float32 [2, 16, 28672], P(None, None, ('col', 'row')), may hold values from -2.4 to 2.4
- up_second_moment: float32 [2, 16, 28672], P(None, None, ('col', 'row')), may hold values from 1 to 50
Outputs:
- hidden: bfloat16 [256, 28672], P('row', 'col')
- token_input_gradient: bfloat16 [256, 16384], P('col', 'row')
- updated_down_factor: float32 [2, 16384, 16], P(None, ('row', 'col'))
- updated_up_factor: float32 [2, 16, 28672], P(None, None, ('col', 'row'))
- updated_down_first_moment: float32 [2, 16384, 16], P(None, ('row', 'col'))
- updated_down_second_moment: float32 [2, 16384, 16], P(None, ('row', 'col'))
- updated_up_first_moment: float32 [2, 16, 28672], P(None, None, ('col', 'row'))
- updated_up_second_moment: float32 [2, 16, 28672], P(None, None, ('col', 'row'))
All inputs are finite; a program needn't handle non-finite values.
Results may differ from a plain program's by a relative error of at most 0.017.
Values may be sent and summed in bfloat16 or wider, within the bound.
A program may use at most 64 MiB of HBM per device.

v0:
```python
import jax
import jax.numpy as jnp
from jax import lax
from jax.sharding import PartitionSpec as P

adapter_scale = 0.5
beta_one = 0.9
beta_two = 0.999
epsilon = 1e-08
learn_rate = 0.001
adam_step = 10.0
highest_precision = lax.Precision.HIGHEST


def moment_optimizer_update(param, moment, second, gradient):
    moment_new = beta_one * moment + (1.0 - beta_one) * gradient
    second_new = beta_two * second + (1.0 - beta_two) * gradient * gradient
    update = (
        moment_new
        / (1.0 - beta_one**adam_step)
        / (jnp.sqrt(second_new / (1.0 - beta_two**adam_step)) + epsilon)
    )
    return (param - learn_rate * update, moment_new, second_new)


def swiglu_pair(projected_tokens, low_local, factor_column_count, cotangent):
    projected_tokens = projected_tokens + adapter_scale * jnp.einsum(
        "ktr,krf->tkf",
        low_local.astype(jnp.float32),
        factor_column_count.astype(jnp.float32),
        precision=highest_precision,
    )
    gate_branch = projected_tokens[:, 0]
    up_projection = projected_tokens[:, 1]
    gate_sig = jax.nn.sigmoid(gate_branch)
    gate_silu = gate_branch * gate_sig
    hidden = (gate_silu * up_projection).astype(jnp.bfloat16)
    grad_out = cotangent.astype(jnp.float32)
    d_gate = (grad_out * up_projection * gate_sig * (1.0 + gate_branch * (1.0 - gate_sig))).astype(
        jnp.bfloat16
    )
    d_upper = (grad_out * gate_silu).astype(jnp.bfloat16)
    return (hidden, jnp.stack([d_gate, d_upper], axis=1))


def per_device(
    tokens,
    cotangent,
    weights,
    adapter_down_master,
    adapter_up_master,
    down_first_moment,
    down_second_moment,
    up_first_moment,
    up_second_moment,
):
    single_float = jnp.float32
    token_panel, a_panel = (
        lax.all_gather(tokens, "col", axis=0, tiled=True),
        lax.all_gather(adapter_down_master.astype(jnp.bfloat16), "col", axis=1, tiled=True),
    )
    factor_column_count = lax.all_gather(
        adapter_up_master.astype(jnp.bfloat16), "row", axis=2, tiled=True
    )
    low_term = jnp.einsum("td,kdr->ktr", token_panel, a_panel, preferred_element_type=single_float)
    tok_rows = cotangent.shape[0]
    offset = lax.axis_index("row") * tok_rows
    row_block = token_panel
    projected_tokens = lax.psum_scatter(
        jnp.einsum("td,kdf->tkf", row_block, weights, preferred_element_type=single_float),
        "row",
        scatter_dimension=0,
        tiled=True,
    )
    low_rank = lax.psum(low_term, "row")
    reduced_half_rows = low_rank.astype(jnp.bfloat16)
    low_local = lax.dynamic_slice_in_dim(reduced_half_rows, offset, tok_rows, 1)
    hidden, d_local = swiglu_pair(projected_tokens, low_local, factor_column_count, cotangent)
    d_whole = lax.all_gather(d_local, "row", axis=0, tiled=True)
    grad_factor = jnp.einsum(
        "tkf,krf->ktr", d_whole, factor_column_count, preferred_element_type=single_float
    )
    a_float = a_panel.astype(single_float)
    row_block = d_whole
    dense_contribution = jnp.einsum(
        "tkf,kdf->td", row_block, weights, preferred_element_type=single_float
    )
    adapter_contribution = jnp.einsum(
        "ktr,kdr->td", grad_factor, a_float, precision=highest_precision
    )
    token_input_gradient = lax.psum_scatter(
        (dense_contribution + adapter_scale * adapter_contribution).astype(jnp.bfloat16),
        "col",
        scatter_dimension=0,
        tiled=True,
    )
    down_partial_sum = adapter_scale * jnp.einsum(
        "up,quv->qpv", token_panel.astype(single_float), grad_factor, precision=highest_precision
    )
    down_factor_gradient = lax.psum_scatter(
        down_partial_sum.astype(jnp.bfloat16), "col", scatter_dimension=1, tiled=True
    ).astype(jnp.float32)
    low_local_b = lax.dynamic_slice_in_dim(reduced_half_rows, offset, tok_rows, 1)
    d_local_b = lax.dynamic_slice_in_dim(d_whole, offset, tok_rows, 0)
    up_partial_sum = adapter_scale * jnp.einsum(
        "dzv,zdh->dvh",
        low_local_b.astype(single_float),
        d_local_b.astype(single_float),
        precision=highest_precision,
    )
    up_factor_gradient = lax.psum_scatter(
        up_partial_sum.astype(jnp.bfloat16), "row", scatter_dimension=2, tiled=True
    ).astype(jnp.float32)
    updated_down_factor, updated_down_first_moment, updated_down_second_moment = (
        moment_optimizer_update(
            adapter_down_master, down_first_moment, down_second_moment, down_factor_gradient
        )
    )
    updated_up_factor, updated_up_first_moment, updated_up_second_moment = moment_optimizer_update(
        adapter_up_master, up_first_moment, up_second_moment, up_factor_gradient
    )
    return (
        hidden,
        token_input_gradient,
        updated_down_factor,
        updated_up_factor,
        updated_down_first_moment,
        updated_down_second_moment,
        updated_up_first_moment,
        updated_up_second_moment,
    )


def solution(mesh):
    placed = (
        P("col", "row"),
        P("row", "col"),
        P(None, "row", "col"),
        P(None, ("row", "col"), None),
        P(None, None, ("col", "row")),
        P(None, ("row", "col"), None),
        P(None, ("row", "col"), None),
        P(None, None, ("col", "row")),
        P(None, None, ("col", "row")),
    )
    return jax.shard_map(
        per_device,
        mesh=mesh,
        in_specs=placed,
        out_specs=(
            P("row", "col"),
            P("col", "row"),
            P(None, ("row", "col"), None),
            P(None, None, ("col", "row")),
            P(None, ("row", "col"), None),
            P(None, ("row", "col"), None),
            P(None, None, ("col", "row")),
            P(None, None, ("col", "row")),
        ),
        check_vma=False,
    )
```

profile of v0, /device:TPU:1, one launch (start us, length us, event | category | flops | bytes accessed | tf_op | source)
XLA Modules:
  0.0 643.9 jit_solution(8913632942395704343)
XLA Ops:
  7.2 39.8 %all_gather.12 = bf16[256,1024]{1,0:T(8,128)(2,1)S(1)} all-gather(bf16[8,1024]{1,0:T(8,128)(2,1)} %param.9), channel_id=1, replica_groups=mesh['row'=16,'col'=32] {'col'}, dimensions={0}, use_global_device_ids=true | all-gather | bytes 540672 | tf_op jit(solution)/shard_map/all_gather | solution.py:59
  47.0 4.4 fusion.10
  51.8 36.4 %all_gather.14 = bf16[2,16,896]{1,0,2:T(2,128)(2,1)S(1)} all-gather(bf16[2,16,56]{1,0,2:T(2,128)(2,1)S(1)} %copy.27), channel_id=1, replica_groups=mesh['row'=16,'col'=32] {'row'}, dimensions={2}, use_global_device_ids=true | all-gather | bytes 60928 | tf_op jit(solution)/shard_map/all_gather | solution.py:62
  88.2 0.6 copy.29
  88.8 38.3 %all_gather.13 = bf16[2,1024,16]{2,0,1:T(2,128)(2,1)S(1)} all-gather(bf16[2,32,16]{2,0,1:T(2,128)(2,1)S(1)} %copy.25), channel_id=1, replica_groups=mesh['row'=16,'col'=32] {'col'}, dimensions={1}, use_global_device_ids=true | all-gather | bytes 67584 | tf_op jit(solution)/shard_map/all_gather | solution.py:60
  127.2 0.3 copy.26
  127.5 0.3 convolution_bitcast_fusion.2
  127.7 52.2 %psum.7 = bf16[2,256,16]{1,2,0:T(8,128)(2,1)S(1)} all-reduce(f32[2,256,16]{1,2,0:T(8,128)S(1)} %convolution_bitcast_fusion.2), channel_id=1, replica_groups=mesh['row'=16,'col'=32] {'row'}, use_global_device_ids=true, to_apply=%region_1.0 | all-reduce | flops 8192 | bytes 49152 | tf_op jit(solution)/shard_map/psum | solution.py:75
  179.9 1.2 fusion.4
  181.1 0.7 fusion.19
  181.8 20.7 %all_gather.15 = bf16[256,2,896]{2,0,1:T(8,128)(2,1)S(1)} all-gather(bf16[16,2,896]{2,0,1:T(8,128)(2,1)S(1)} %pad_maximum_fusion), channel_id=1, replica_groups=mesh['row'=16,'col'=32] {'row'}, dimensions={0}, use_global_device_ids=true | all-gather | bytes 974848 | tf_op jit(solution)/shard_map/all_gather | solution.py:79
  202.4 0.3 fusion.30
  202.8 3.2 convolution_bitcast_fusion.1
  206.0 0.4 fusion.7
  206.4 0.4 copy.33
  206.8 0.9 reshape.19
  207.8 1.4 fusion.2
  209.3 1.3 dynamic-slice
  211.4 44.8 %all-reduce = bf16[2,16,896]{2,1,0:T(8,128)(2,1)S(1)} all-reduce(bf16[2,16,896]{2,1,0:T(8,128)(2,1)S(1)} %fusion.6), channel_id=5, replica_groups=mesh['row'=16,'col'=32] {'row'}, use_global_device_ids=true, to_apply=%region_4.0.clone | all-reduce | flops 28672 | bytes 114688
  256.2 0.7 multiply_subtract_fusion
  256.9 158.3 %reduce-scatter.11.cloned.1.call-done = bf16[32,32]{1,0:T(8,128)(2,1)} async-done(((bf16[1024,32]{1,0:T(8,128)(2,1)}), bf16[32,32]{1,0:T(8,128)(2,1)}) %reduce-scatter.11.cloned.1.call-update) | async-done | bytes 2064
  415.2 0.8 reshape.20
  416.0 0.6 multiply_subtract_fusion.1
  416.7 220.7 %reduce-scatter.9.cloned.1.call-done = bf16[8,1024]{1,0:T(8,128)(2,1)} async-done(((bf16[256,1024]{1,0:T(8,128)(2,1)}), bf16[8,1024]{1,0:T(8,128)(2,1)}) %reduce-scatter.9.cloned.1.call-update) | async-done | bytes 16400 | tf_op jit(solution)/shard_map/reduce_scatter | solution.py:91
  (28 shorter events, 0.7 us)
Async XLA Ops:
  7.2 172.7 %reduce-scatter.7.cloned.1.call-start = ((), (), s32[]{:S(2)}) async-start(), calls=%async_computation.3 | async-start | bytes 1949696 | tf_op jit(solution)/shard_map/reduce_scatter | solution.py:69
  47.0 4.5 copy-start.1
  47.0 4.6 copy-start
  51.5 129.6 %copy-start.2 = (bf16[16,896]{1,0:T(8,128)(2,1)S(1)}, bf16[16,896]{1,0:T(8,128)(2,1)}, u32[]{:S(2)}) copy-start(bf16[16,896]{1,0:T(8,128)(2,1)} %param.10) | copy-start | bytes 86020
  51.5 363.7 %reduce-scatter.11.cloned.1.call-start = ((), (), s32[]{:S(2)}) async-start(), calls=%async_computation.5 | async-start | bytes 270336
  206.0 50.2 %copy-start.3 = (f32[2,16,56]{2,1,0:T(8,128)S(1)}, f32[2,16,56]{2,1,0:T(8,128)}, u32[]{:S(2)}) copy-start(f32[2,16,56]{2,1,0:T(8,128)} %param.16) | copy-start | bytes 21508
  206.0 50.2 %copy-start.4 = (f32[2,16,56]{2,1,0:T(8,128)S(1)}, f32[2,16,56]{2,1,0:T(8,128)}, u32[]{:S(2)}) copy-start(f32[2,16,56]{2,1,0:T(8,128)} %param.17) | copy-start | bytes 21508
  206.0 210.0 %copy-start.5 = (f32[2,32,16]{1,2,0:T(8,128)S(1)}, f32[2,32,16]{1,2,0:T(8,128)}, u32[]{:S(2)}) copy-start(f32[2,32,16]{1,2,0:T(8,128)} %param.14) | copy-start | bytes 12292
  206.0 210.0 %copy-start.6 = (f32[2,32,16]{1,2,0:T(8,128)S(1)}, f32[2,32,16]{1,2,0:T(8,128)}, u32[]{:S(2)}) copy-start(f32[2,32,16]{1,2,0:T(8,128)} %param.15) | copy-start | bytes 12292
  207.7 429.7 %reduce-scatter.9.cloned.1.call-start = ((), (), s32[]{:S(2)}) async-start(), calls=%async_computation.4 | async-start | bytes 540672 | tf_op jit(solution)/shard_map/reduce_scatter | solution.py:91
Sparse Core Ops, SparseCore 0:
  51.6 72.6 reduce-scatter.6
  207.9 207.2 reduce-scatter.10
  420.1 217.2 reduce-scatter.8
where the time goes:
time: 649 us; the launch traced here: 644 us
  waiting for transfers between devices  379 us (58%)
  blocking collectives  232 us (36%)
  between operations  14.6 us (2%)
  matrix products  11.4 us (2%)
    reduce_scatter x1, waiting for transfers between devices, per_device(): lax.psum_scatter((dense_contribution + adapter_scale * adapter_contributi...  221 us
    unnamed x4, waiting for transfers between devices  158 us
    psum x1, blocking collectives, per_device(): low_rank = lax.psum(low_term, 'row')  52.2 us
    unnamed x1, blocking collectives  44.8 us
    all_gather x1, blocking collectives, per_device(): lax.all_gather(tokens, 'col', axis=0, tiled=True)  39.8 us
    all_gather x1, blocking collectives, per_device(): lax.all_gather(adapter_down_master.astype(jnp.bfloat16), 'col', axis=1, t...  38.3 us
    all_gather x1, blocking collectives, per_device(): lax.all_gather(adapter_up_master.astype(jnp.bfloat16), 'row', axis=2, til...  36.4 us
    all_gather x1, blocking collectives, per_device(): d_whole = lax.all_gather(d_local, 'row', axis=0, tiled=True)  20.7 us
  transfers between devices with their start and end apart: 3, of which 2 were waited for; matrix products, arithmetic and copies ran while one was open for 1% of the time, Pallas kernels for 0%

commit v1 on v0

v1 whole, which is shorter than its diff:
```python
import jax
import jax.numpy as jnp
from jax import lax
from jax.experimental import pallas as pl
from jax.experimental.pallas import tpu as pltpu
from jax.sharding import PartitionSpec as P

F32 = jnp.float32
BF16 = jnp.bfloat16
MESH = pl.DeviceIdType.MESH
adapter_scale = 0.5
beta_one = 0.9
beta_two = 0.999
epsilon = 1e-08
learn_rate = 0.001
adam_step = 10.0

NX, NY, NZ, NC = 4, 8, 8, 2
ROWS, COLS = NZ * NC, NX * NY
NEAR_LAST = (4, 3, 5, 2, 6, 1, 7)
NEAR_FIRST = (1, 7, 2, 6, 3, 5, 4)
NT = (((1,), (1,)), ((), ()))


def adam(param, moment, second, gradient):
    moment_new = beta_one * moment + (1.0 - beta_one) * gradient
    second_new = beta_two * second + (1.0 - beta_two) * gradient * gradient
    update = (
        moment_new
        / (1.0 - beta_one**adam_step)
        / (jnp.sqrt(second_new / (1.0 - beta_two**adam_step)) + epsilon)
    )
    return (param - learn_rate * update, moment_new, second_new)


def dot(a, b):
    return jnp.dot(a, b, preferred_element_type=F32)


def kernel(
    tok_h, cot_h, w_h, a_h, b_h, ma_h, va_h, mb_h, vb_h,
    hid_o, dx_o, pa_o, pb_o, mao_o, vao_o, mbo_o, vbo_o,
    tok, cot, w, a, b, ma, va, mb, vb,
    tblk, aw, bw, bblk, bf, bb, x, a4, s1, r1, y, s2, r2, d, s3, r3, s4, r4,
    in_sem, t_send, t_recv, b_send, b_recv, f_send, f_recv, d_send, d_recv, g_send, g_recv,
):
    row, col = lax.axis_index("row"), lax.axis_index("col")
    z, c = row // NC, row % NC
    px, py = col // NY, col % NY
    oc = 1 - c

    def at_z(off):
        return (lax.rem(z + off, NZ) * NC + c, col)

    partner = (z * NC + oc, col)

    def at_y(off):
        return (row, px * NY + lax.rem(py + off, NY))

    def at_x(off):
        return (row, lax.rem(px + off, NX) * NY + py)

    def at_row(off):
        return (lax.rem(row + off, ROWS), col)

    def remote(src, dst, send, recv, to):
        return pltpu.make_async_remote_copy(
            src_ref=src, dst_ref=dst, send_sem=send, recv_sem=recv, device_id=to, device_id_type=MESH
        )

    loads = [
        pltpu.make_async_copy(h, v, in_sem.at[i])
        for i, (h, v) in enumerate(
            [(tok_h, tok), (a_h, a), (b_h, b), (w_h, w), (cot_h, cot), (ma_h, ma), (va_h, va), (mb_h, mb), (vb_h, vb)]
        )
    ]
    for load in loads:
        load.start()

    barrier = pltpu.get_barrier_semaphore()
    greet = (
        [at_y(o) for o in range(1, NY)] + [at_x(o) for o in range(1, NX)] + [at_row(o) for o in range(1, ROWS)]
    )
    for peer in greet:
        pl.semaphore_signal(barrier, inc=1, device_id=peer, device_id_type=MESH)

    for load in loads[:3]:
        load.wait()
    t = tok[...].astype(F32)
    for k in range(2):
        for j in range(4):
            aw[:, 32 * j + 16 * k : 32 * j + 16 * k + 16] = a[k, 8 * j : 8 * j + 8, :]
    tblk[col, :, 0:512] = jnp.concatenate([t[:, :512], t[:, 512:]], axis=0).astype(BF16)
    tblk[col, :, 512:640] = jnp.concatenate([aw[...], jnp.zeros((8, 128), F32)], axis=0).astype(BF16)
    bw[...] = jnp.zeros((32, 128), F32)
    for k in range(2):
        bw[16 * k : 16 * k + 16, 0:56] = b[k]
    bblk[row] = bw[...].astype(BF16)

    pl.semaphore_wait(barrier, len(greet))

    sends = []

    def go(copy):
        copy.start()
        sends.append(copy)

    for o in NEAR_LAST:
        go(remote(tblk.at[col], tblk.at[col], t_send.at[o], t_recv.at[o], at_y(o)))

    def spread_x(yo):
        src = px * NY + lax.rem(py - yo + NY, NY)
        for o in (2, 1, 3):
            i = o * NY + yo
            go(remote(tblk.at[src], tblk.at[src], t_send.at[i], t_recv.at[i], at_x(o)))

    spread_x(0)
    for o in range(1, ROWS):
        go(remote(bblk.at[row], bblk.at[row], b_send.at[o], b_recv.at[o], at_row(o)))
    for o in NEAR_FIRST:
        remote(tblk.at[col], tblk.at[col], t_send.at[o], t_recv.at[o], at_y(o)).wait_recv()
        spread_x(o)

    for o in range(1, ROWS):
        remote(bblk.at[row], bblk.at[row], b_send.at[o], b_recv.at[o], at_row(o)).wait_recv()
    for r in range(ROWS):
        bf[:, 56 * r : 56 * r + 56] = bblk[r].astype(F32)[:, 0:56]
    bfull = bf[...].astype(BF16)
    zero = jnp.zeros((16, 896), BF16)
    for j in range(4):
        for k in range(2):
            g = 32 * j + 16 * k
            bb[g : g + 16, 896 * k : 896 * k + 896] = bfull[16 * k : 16 * k + 16]
            bb[g : g + 16, 896 * (1 - k) : 896 * (1 - k) + 896] = zero

    for yo in range(NY):
        for o in (1, 3, 2):
            i = o * NY + yo
            remote(tblk.at[col], tblk.at[col], t_send.at[i], t_recv.at[i], at_x(o)).wait_recv()

    v = tblk[...].astype(F32)
    v5 = v.reshape(NZ, NC, 2, 16, 640)
    for cc in range(NC):
        u = v5[:, cc].reshape(16, 16, 640)
        x[cc, :, 0:512] = u[:, :8, :512].reshape(128, 512).astype(BF16)
        x[cc, :, 512:1024] = u[:, 8:, :512].reshape(128, 512).astype(BF16)
    group = lax.broadcasted_iota(jnp.int32, (COLS, 4, 8, 128), 3) // 32
    which = lax.broadcasted_iota(jnp.int32, (COLS, 4, 8, 128), 1)
    arep = jnp.broadcast_to(v[:, None, :8, 512:640], (COLS, 4, 8, 128))
    a4[...] = jnp.where(group == which, arep, 0.0).reshape(1024, 128).astype(BF16)

    loads[3].wait()
    xo = x[oc]
    s1[:, :, 0:896] = dot(xo, w[0]).astype(BF16).reshape(NZ, 16, 896)
    s1[:, :, 896:1792] = dot(xo, w[1]).astype(BF16).reshape(NZ, 16, 896)
    s1[:, :, 1792:1920] = dot(xo, a4[...]).astype(BF16).reshape(NZ, 16, 128)
    core_sum = remote(s1, r1, f_send.at[0], f_recv.at[0], partner)
    go(core_sum)
    xm = x[c]
    y[:, :, 0:896] = dot(xm, w[0]).reshape(NZ, 16, 896)
    y[:, :, 896:1792] = dot(xm, w[1]).reshape(NZ, 16, 896)
    y[:, :, 1792:1920] = dot(xm, a4[...]).reshape(NZ, 16, 128)
    core_sum.wait_recv()
    for o in NEAR_LAST:
        to = lax.rem(z + o, NZ)
        s2[to] = (y[to] + r1[to].astype(F32)).astype(BF16)
        go(remote(s2.at[to], r2.at[o], f_send.at[o], f_recv.at[o], at_z(o)))
    total = y[z] + r1[z].astype(F32)
    for load in loads[4:]:
        load.wait()
    for o in NEAR_FIRST:
        remote(s2.at[z], r2.at[o], f_send.at[o], f_recv.at[o], at_z(o)).wait_recv()
        total = total + r2[o].astype(F32)

    low = total[:, 1792:]
    low = low + pltpu.roll(low, 64, 1)
    low = low + pltpu.roll(low, 32, 1)
    lane = lax.broadcasted_iota(jnp.int32, (16, 128), 1)
    low_half = jnp.where(lane < 32, low, 0.0).astype(BF16)
    both = total[:, :1792] + adapter_scale * dot(low_half, bb[...])
    gate, up = both[:, :896], both[:, 896:]
    sig = jax.nn.sigmoid(gate)
    silu = gate * sig
    grad = cot[...].astype(F32)
    hid_o[...] = (silu * up).astype(BF16)
    d[c, z, :, 0:896] = (grad * up * sig * (1.0 + gate * (1.0 - sig))).astype(BF16)
    d[c, z, :, 896:1792] = (grad * silu).astype(BF16)
    d[c, z, :, 1792:1920] = low_half

    for o in NEAR_LAST:
        go(remote(d.at[c, z], d.at[c, z], d_send.at[o], d_recv.at[o], at_z(o)))
    go(remote(d.at[c, z], d.at[c, z], d_send.at[0], d_recv.at[0], partner))
    for o in NEAR_FIRST:
        remote(d.at[c, z], d.at[c, z], d_send.at[o], d_recv.at[o], at_z(o)).wait_recv()
        src = lax.rem(z - o + NZ, NZ)
        go(remote(d.at[c, src], d.at[c, src], d_send.at[8 + o], d_recv.at[8 + o], partner))
    remote(d.at[c, z], d.at[c, z], d_send.at[0], d_recv.at[0], partner).wait_recv()
    for o in NEAR_FIRST:
        remote(d.at[c, z], d.at[c, z], d_send.at[8 + o], d_recv.at[8 + o], partner).wait_recv()

    dall = d[...].reshape(256, 1920)
    dg, du = dall[:, :896], dall[:, 896:1792]
    fac = lax.dot_general(dall[:, :1792], bb[...], NT, preferred_element_type=F32)
    fac = adapter_scale * fac
    fac_half = fac.astype(BF16)
    dx = lax.dot_general(dg, w[0], NT, preferred_element_type=F32)
    dx = dx + lax.dot_general(du, w[1], NT, preferred_element_type=F32)
    dx = dx + lax.dot_general(fac_half, a4[...], NT, preferred_element_type=F32)
    xall = x[...].reshape(256, 1024)
    ga = dot(fac.T.astype(BF16), xall).T.reshape(COLS, 4, 8, 128)
    ga = jnp.sum(jnp.where(group == which, ga, 0.0), axis=1)
    dx6 = dx.reshape(NC, NX, 2, 2, 8, 1024)
    for yy in range(NY):
        blk = dx6[(yy // 2) % 2, :, yy // 4, yy % 2]
        s3[:, yy, :, 0:512] = jnp.concatenate([blk[:, :, :512], blk[:, :, 512:]], axis=1)
    ga4 = ga.reshape(NX, NY, 8, 128)
    s3[:, :, :, 512:640] = jnp.concatenate([ga4, jnp.zeros_like(ga4)], axis=2)
    for o in (2, 1, 3):
        to = lax.rem(px + o, NX)
        s4[o] = s3[to].astype(BF16)
        go(remote(s4.at[o], r3.at[o], g_send.at[o], g_recv.at[o], at_x(o)))

    low_t = dall[:, 1792:].astype(F32).T[:32].astype(BF16)
    gb = adapter_scale * dot(low_t, dall[:, :1792])
    shift = lax.rem(896 - 56 * row, 896)
    for k in range(2):
        gk = pltpu.roll(gb[16 * k : 16 * k + 16, 896 * k : 896 * k + 896], shift, 1)[:, :56]
        pb_o[k], mbo_o[k], vbo_o[k] = adam(b[k], mb[k], vb[k], gk)

    part = s3[px]
    for o in (1, 3, 2):
        remote(s4.at[o], r3.at[o], g_send.at[o], g_recv.at[o], at_x(o)).wait_recv()
        part = part + r3[o].astype(F32)
    s3[px] = part
    s4[0] = part.astype(BF16)
    for o in NEAR_LAST:
        to = lax.rem(py + o, NY)
        go(remote(s4.at[0, to], r4.at[o], g_send.at[3 + o], g_recv.at[3 + o], at_y(o)))
    last = s3[px, py]
    for o in NEAR_FIRST:
        remote(s4.at[0, 0], r4.at[o], g_send.at[3 + o], g_recv.at[3 + o], at_y(o)).wait_recv()
        last = last + r4[o].astype(F32)
    dx_o[:, 0:512] = last[:8, :512].astype(BF16)
    dx_o[:, 512:1024] = last[8:, :512].astype(BF16)
    for k in range(2):
        for j in range(4):
            rows = slice(8 * j, 8 * j + 8)
            lanes = 512 + 32 * j + 16 * k
            gk = last[:8, lanes : lanes + 16]
            pa_o[k, rows, :], mao_o[k, rows, :], vao_o[k, rows, :] = adam(
                a[k, rows, :], ma[k, rows, :], va[k, rows, :], gk
            )
    for copy in sends:
        copy.wait_send()


def per_device(*args):
    tok, cot, w, a, b, ma, va, mb, vb = args
    outs = (
        jax.ShapeDtypeStruct(cot.shape, BF16),
        jax.ShapeDtypeStruct(tok.shape, BF16),
        jax.ShapeDtypeStruct(a.shape, F32),
        jax.ShapeDtypeStruct(b.shape, F32),
        jax.ShapeDtypeStruct(a.shape, F32),
        jax.ShapeDtypeStruct(a.shape, F32),
        jax.ShapeDtypeStruct(b.shape, F32),
        jax.ShapeDtypeStruct(b.shape, F32),
    )
    vmem, dma = pltpu.VMEM, pltpu.SemaphoreType.DMA
    return pl.pallas_call(
        kernel,
        out_shape=outs,
        in_specs=[pl.BlockSpec(memory_space=pl.ANY)] * 9,
        out_specs=[pl.BlockSpec(memory_space=pltpu.VMEM)] * 8,
        scratch_shapes=[vmem(v.shape, v.dtype) for v in args]
        + [
            vmem((COLS, 16, 640), BF16),
            vmem((8, 128), F32),
            vmem((32, 128), F32),
            vmem((ROWS, 32, 128), BF16),
            vmem((32, 896), F32),
            vmem((128, 1792), BF16),
            vmem((NC, 128, 1024), BF16),
            vmem((1024, 128), BF16),
            vmem((NZ, 16, 1920), BF16),
            vmem((NZ, 16, 1920), BF16),
            vmem((NZ, 16, 1920), F32),
            vmem((NZ, 16, 1920), BF16),
            vmem((NZ, 16, 1920), BF16),
            vmem((NC, NZ, 16, 1920), BF16),
            vmem((NX, NY, 16, 640), F32),
            vmem((NX, NY, 16, 640), BF16),
            vmem((NX, NY, 16, 640), BF16),
            vmem((NY, 16, 640), BF16),
            dma((9,)),
            dma((COLS,)), dma((COLS,)),
            dma((ROWS,)), dma((ROWS,)),
            dma((NZ,)), dma((NZ,)),
            dma((ROWS,)), dma((ROWS,)),
            dma((11,)), dma((11,)),
        ],
        compiler_params=pltpu.CompilerParams(
            collective_id=0, has_side_effects=True, vmem_limit_bytes=48 * 1024 * 1024
        ),
    )(*args)


def solution(mesh):
    placed = (
        P("col", "row"),
        P("row", "col"),
        P(None, "row", "col"),
        P(None, ("row", "col"), None),
        P(None, None, ("col", "row")),
        P(None, ("row", "col"), None),
        P(None, ("row", "col"), None),
        P(None, None, ("col", "row")),
        P(None, None, ("col", "row")),
    )
    return jax.shard_map(
        per_device,
        mesh=mesh,
        in_specs=placed,
        out_specs=(
            P("row", "col"),
            P("col", "row"),
            P(None, ("row", "col"), None),
            P(None, None, ("col", "row")),
            P(None, ("row", "col"), None),
            P(None, ("row", "col"), None),
            P(None, None, ("col", "row")),
            P(None, None, ("col", "row")),
        ),
        check_vma=False,
    )
```

time: 649 us -> 92.1 us (0.14)
  waiting for transfers between devices: 379 us -> 0 us
  blocking collectives: 232 us -> 0 us
  Pallas kernels: 0 us -> 77.6 us
  between operations: 14.6 us -> 0.65 us
  matrix products: 11.4 us -> 0 us
  local copies, waits for them, and re-layouts: 4.64 us -> 13.1 us
    reduce_scatter x2 -> x0, waiting for transfers between devices: 221 us -> none  [the longest x1 221 us: per_device(): lax.psum_scatter((dense_contribution + adapter_scale * adapter_contributi...]
    unnamed x4 -> x0, waiting for transfers between devices: 158 us -> none
    all_gather x4 -> x0, blocking collectives: 135 us -> none  [the longest x1 39.8 us: per_device(): lax.all_gather(tokens, 'col', axis=0, tiled=True)]
    pallas_call x0 -> x1, Pallas kernels: none -> 77.6 us  [per_device(): pl.pallas_call(kernel, out_shape=outs, in_specs=[pl.BlockSpec(memory_spac...]
    psum x1 -> x0, blocking collectives: 52.2 us -> none  [per_device(): low_rank = lax.psum(low_term, 'row')]
    unnamed x1 -> x0, blocking collectives: 44.8 us -> none
    dot_general x8 -> x0, matrix products: 11.4 us -> none  [the longest x1 4.43 us: per_device(): jnp.einsum('td,kdf->tkf', row_block, weights, preferred_element_type=sing...]
    unnamed x19 -> x20, local copies, waits for them, and re-layouts: 3.49 us -> 11.1 us
  transfers between devices with their start and end apart: 3 -> 0, of which waited for: 2 -> 0; matrix products, arithmetic and copies ran while one was open for 1% -> 0% of each run, Pallas kernels for 0% -> 0%
where the time goes in v1:
time: 92.1 us; the launch traced here: 91.4 us
  Pallas kernels  77.6 us (84%)
  local copies, waits for them, and re-layouts  13.1 us (14%)
    pallas_call x1, Pallas kernels, per_device(): pl.pallas_call(kernel, out_shape=outs, in_specs=[pl.BlockSpec(memory_spac...  77.6 us
    unnamed x20, local copies, waits for them, and re-layouts  11.1 us
    pallas_call x3, local copies, waits for them, and re-layouts, per_device(): pl.pallas_call(kernel, out_shape=outs, in_specs=[pl.BlockSpec(memory_spac...  2.03 us

profile of v1, /device:TPU:1, one launch (start us, length us, event | category | flops | bytes accessed | tf_op | source)
XLA Modules:
  0.0 91.4 jit_solution(4654771331752547562)
XLA Ops:
  0.6 0.8 copy.17.a_h
  1.4 0.8 copy.18.ma_h
  2.2 0.8 copy.19.va_h
  3.0 0.0 copy-start
  3.0 2.0 %copy-done = bf16[2,1024,896]{2,1,0:T(8,128)(2,1)S(1)} copy-done((bf16[2,1024,896]{2,1,0:T(8,128)(2,1)S(1)}, bf16[2,1024,896]{2,1,0:T(8,128)(2,1)}, u32[]{:S(2)}) %copy-start) | copy-done | bytes 3670040
  5.0 0.0 copy-start.1
  5.1 0.7 copy-done.1
  5.8 0.0 copy-start.2
  5.8 0.7 copy-done.2
  6.5 0.0 copy-start.3
  6.5 0.7 copy-done.3
  7.2 0.0 copy-start.4
  7.2 0.7 copy-done.4
  8.0 0.0 copy-start.5
  8.0 0.7 copy-done.5
  8.7 77.6 %shard_map.152 = (bf16[16,896]{1,0:T(8,128)(2,1)S(1)}, bf16[8,1024]{1,0:T(8,128)(2,1)S(1)}, f32[2,32,16]{2,1,0:T(8,128)S(1)}, f32[2,16,56]{2,1,0:T(8,128)S(1)}, ...) custom-call(bf16[8,1024]{1,0:T(8,128)(2,1)S(1)} %copy-done.2, ...), custom_call_target="tpu_custom_call" | custom-call | tf_op jit(solution)/shard_map/pallas_call | solution.py:270
  86.3 0.7 copy.20
  87.0 0.7 copy.21
  87.7 0.7 copy.22
  88.3 0.6 copy.28
  88.9 0.6 copy.29
  89.5 0.6 copy.30
  90.1 0.6 copy.31
  90.8 0.6 copy.32
Async XLA Ops:
  3.0 2.0 %copy-start = (bf16[2,1024,896]{2,1,0:T(8,128)(2,1)S(1)}, bf16[2,1024,896]{2,1,0:T(8,128)(2,1)}, u32[]{:S(2)}) copy-start(bf16[2,1024,896]{2,1,0:T(8,128)(2,1)} %w_h.1) | copy-start | bytes 11010052
  5.0 0.7 copy-start.1
  5.8 0.7 copy-start.2
  6.5 0.7 copy-start.3
  7.2 0.7 copy-start.4
  8.0 0.7 copy-start.5

commit v2 on v1

v2 whole, which is shorter than its diff:
```python
import jax
import jax.numpy as jnp
from jax import lax
from jax.experimental import pallas as pl
from jax.experimental.pallas import tpu as pltpu
from jax.sharding import PartitionSpec as P

F32 = jnp.float32
BF16 = jnp.bfloat16
MESH = pl.DeviceIdType.MESH
adapter_scale = 0.5
beta_one = 0.9
beta_two = 0.999
epsilon = 1e-08
learn_rate = 0.001
adam_step = 10.0

NX, NY, NZ, NC = 4, 8, 8, 2
ROWS, COLS = NZ * NC, NX * NY
HID = 896
WIDTH = (HID, HID + 128)
FAR_FIRST = (4, 3, 5, 2, 6, 1, 7)
NT = (((1,), (1,)), ((), ()))


def adam(param, moment, second, gradient):
    moment_new = beta_one * moment + (1.0 - beta_one) * gradient
    second_new = beta_two * second + (1.0 - beta_two) * gradient * gradient
    update = (
        moment_new
        / (1.0 - beta_one**adam_step)
        / (jnp.sqrt(second_new / (1.0 - beta_two**adam_step)) + epsilon)
    )
    return (param - learn_rate * update, moment_new, second_new)


def dot(a, b):
    return jnp.dot(a, b, preferred_element_type=F32)


def kernel(
    tok_h, cot_h, w_h, a_h, b_h, ma_h, va_h, mb_h, vb_h,
    hid_o, dx_o, pa_o, pb_o, mao_o, vao_o, mbo_o, vbo_o,
    tok, cot, w, a, b, ma, va, mb, vb,
    hid, dxv, pa, pb, mao, vao, mbo, vbo,
    tblk, aw, bw, bblk, bf, bb, x, af, at, yo, s1, r1, sa, ra, sb, rb, lows, lowr, hidf, d0, d1, fac,
    s3, s4, r3, s5, r5, ga3, ga4, gar, ga5, ga6,
    in_sem, out_sem, t_send, t_recv, b_send, b_recv, c_send, c_recv, a_send, a_recv, f_send, f_recv,
    l_send, l_recv, g_send, g_recv, p_send, p_recv, x_send, x_recv, y_send, y_recv, q_send, q_recv, k_send, k_recv,
):
    d = (d0, d1)
    row, col = lax.axis_index("row"), lax.axis_index("col")
    z, c = row // NC, row % NC
    px, py = col // NY, col % NY
    par = py % 2
    oc = 1 - c
    sgn = 1 - 2 * c

    def zc(off):
        return lax.rem(z + sgn * off + NZ, NZ)

    def at_z(off):
        return (zc(off) * NC + c, col)

    def at_y(off):
        return (row, px * NY + lax.rem(py + off, NY))

    def at_x(off):
        return (row, lax.rem(px + off, NX) * NY + py)

    def at_row(off):
        return (lax.rem(row + off, ROWS), col)

    partner = (z * NC + oc, col)

    def remote(src, dst, send, recv, to):
        return pltpu.make_async_remote_copy(
            src_ref=src, dst_ref=dst, send_sem=send, recv_sem=recv, device_id=to, device_id_type=MESH
        )

    sends = []

    def go(*copy):
        copy = remote(*copy)
        copy.start()
        sends.append(copy)

    loads = [
        pltpu.make_async_copy(h, v, in_sem.at[i])
        for i, (h, v) in enumerate(
            [(tok_h, tok), (a_h, a), (b_h, b), (w_h, w), (cot_h, cot), (ma_h, ma), (va_h, va), (mb_h, mb), (vb_h, vb)]
        )
    ]
    for load in loads:
        load.start()
    outs = [(hid, hid_o), (dxv, dx_o), (pa, pa_o), (pb, pb_o), (mao, mao_o), (vao, vao_o), (mbo, mbo_o), (vbo, vbo_o)]
    stores = [pltpu.make_async_copy(v, h, out_sem.at[i]) for i, (v, h) in enumerate(outs)]

    barrier = pltpu.get_barrier_semaphore()
    greet = (
        [at_y(o) for o in range(1, NY)] + [at_x(o) for o in range(1, NX)] + [at_row(o) for o in range(1, ROWS)]
    )
    for peer in greet:
        pl.semaphore_signal(barrier, inc=1, device_id=peer, device_id_type=MESH)

    def block(xx, yy):
        return tblk.at[2 * xx + yy // 4, (yy // 2) % 2, yy % 2]

    for load in loads[:3]:
        load.wait()
    t = tok[...].astype(F32)
    for k in range(2):
        for h in range(2):
            j = 2 * k + h
            aw[:, 32 * j : 32 * j + 32] = a[k, 8 * h : 8 * h + 8, :]
    own = block(px, py)
    own[:, 0:512] = jnp.concatenate([t[:, :512], t[:, 512:]], axis=0).astype(BF16)
    own[:, 512:640] = jnp.concatenate([aw[...], jnp.zeros((8, 128), F32)], axis=0).astype(BF16)
    bw[...] = jnp.zeros((32, 128), F32)
    for k in range(2):
        bw[16 * k : 16 * k + 16, 0:56] = b[k]
    bblk[row] = bw[...].astype(BF16)

    pl.semaphore_wait(barrier, len(greet))

    for o in FAR_FIRST:
        go(own, own, t_send.at[o], t_recv.at[o], at_y(o))

    def source(g, j):
        return lax.rem(jnp.where(par == g, 0, 1) + (0, 2, 6, 4)[j], NY)

    def spread_copy(g, j, o):
        src = block(px, lax.rem(py - source(g, j) + NY, NY))
        i = 3 * (4 * g + j) + o - 1
        return (src, src, t_send.at[8 + i], t_recv.at[8 + i], at_x(o))

    def spread(g, j):
        off = source(g, j)
        if j == 0:

            @pl.when(off != 0)
            def _():
                remote(own, own, t_send.at[off], t_recv.at[off], at_y(1)).wait_recv()
        else:
            remote(own, own, t_send.at[off], t_recv.at[off], at_y(1)).wait_recv()
        for o in (2, 1, 3):
            go(*spread_copy(g, j, o))

    for o in range(1, ROWS):
        go(bblk.at[row], bblk.at[row], b_send.at[o], b_recv.at[o], at_row(o))
    for j in range(4):
        spread(0, j)
    for j in range(4):
        spread(1, j)

    def take(g):
        for j in range(4):
            for o in (1, 3, 2):
                remote(*spread_copy(g, j, o)).wait_recv()
        for rel in range(2):
            u = tblk[:, oc if rel == 0 else c, g].astype(F32)
            x[g, 64 * rel : 64 * rel + 64, 0:512] = u[:, :8, :512].reshape(64, 512).astype(BF16)
            x[g, 64 * rel : 64 * rel + 64, 512:1024] = u[:, 8:, :512].reshape(64, 512).astype(BF16)

    def core_copy(g):
        return (s1.at[g], r1.at[g], c_send.at[g], c_recv.at[g], partner)

    def forward(g):
        src = x[g]
        gate, up = dot(src, w[0]), dot(src, w[1])
        other = [p[:64].reshape(NZ, 8, HID) for p in (gate, up)]
        s1[g] = jnp.concatenate(other, axis=1).astype(BF16)
        go(*core_copy(g))
        mine = [p[64:].reshape(NZ, 8, HID) for p in (gate, up)]
        yo[g] = jnp.concatenate(mine, axis=1)

    def sum_copy(g, i, to):
        return (sa.at[g, i], ra.at[g, i], a_send.at[5 * g + i], a_recv.at[5 * g + i], at_z(to))

    first = ((4, 2), (3, 1), (-3, -1), (1, 1), (-1, -1))

    def sum_first(g):
        remote(*core_copy(g)).wait_recv()
        yo[g] = yo[g] + r1[g].astype(F32)
        for i, (owner, to) in enumerate(first):
            sa[g, i] = yo[g, zc(owner)].astype(BF16)
            go(*sum_copy(g, i, to))

    def second_copy(g, i):
        return (sb.at[g, i], rb.at[g, i], f_send.at[2 * g + i], f_recv.at[2 * g + i], at_z((2, -2)[i]))

    def sum_second(g):
        remote(*sum_copy(g, 1, 1)).wait_recv()
        remote(*sum_copy(g, 0, 2)).wait_recv()
        sb[g, 0] = (yo[g, zc(2)] + ra[g, 0].astype(F32) + ra[g, 1].astype(F32)).astype(BF16)
        go(*second_copy(g, 0))
        remote(*sum_copy(g, 2, -1)).wait_recv()
        sb[g, 1] = (yo[g, zc(-2)] + ra[g, 2].astype(F32)).astype(BF16)
        go(*second_copy(g, 1))

    def low_copy(o):
        to = lax.rem(row + o, ROWS)
        rel = jnp.where(to % NC == c, 1, 0)
        return (lows.at[rel, to // NC], lowr.at[o], l_send.at[o], l_recv.at[o], (to, col))

    def low_sends():
        both = [
            lax.dot_general(x[g], at[...], NT, preferred_element_type=F32).reshape(NC, NZ, 8, 128) for g in range(2)
        ]
        lows[...] = jnp.concatenate(both, axis=2).astype(BF16)
        for o in range(1, ROWS):
            go(*low_copy(o))

    def low_total():
        total = lows[1, z].astype(F32)
        for o in range(1, ROWS):
            remote(*low_copy(o)).wait_recv()
            total = total + lowr[o].astype(F32)
        keep = lax.broadcasted_iota(jnp.int32, (16, 128), 1) < 32
        return jnp.where(keep, total, 0.0).astype(BF16)

    def pass_copy(g, off, to):
        blk = d[g].at[1, zc(-off)]
        i = 8 * g + (off + to) % 8
        return (blk, blk, g_send.at[i], g_recv.at[i], at_z(to))

    def cross(g, off):
        i = 8 * g + off % 8
        return (d[g].at[1, zc(-off)], d[g].at[0, zc(-off)], p_send.at[i], p_recv.at[i], partner)

    def activate(g, gate_low, up_low, low_half):
        for i in (3, 4):
            remote(*sum_copy(g, i, first[i][1])).wait_recv()
        for i in (0, 1):
            remote(*second_copy(g, i)).wait_recv()
        total = yo[g, z] + ra[g, 3].astype(F32) + ra[g, 4].astype(F32) + rb[g, 0].astype(F32) + rb[g, 1].astype(F32)
        gate = total[:8] + gate_low[8 * g : 8 * g + 8]
        up = total[8:] + up_low[8 * g : 8 * g + 8]
        sig = jax.nn.sigmoid(gate)
        silu = gate * sig
        grad = cot[...].astype(F32)[8 * g : 8 * g + 8]
        d_gate = grad * up * sig * (1.0 + gate * (1.0 - sig))
        d_up = grad * silu
        d[g][1, z, :, 0:HID] = jnp.concatenate([d_gate, d_up], axis=0).astype(BF16)
        if g == 1:
            d[g][1, z, :, HID:] = low_half
        for to in (2, 1, -2, -1):
            go(*pass_copy(g, 0, to))
        go(*cross(g, 0))
        hidf[8 * g : 8 * g + 8, :] = silu * up

    def pass_on(g):
        remote(*pass_copy(g, 0, 1)).wait_recv()
        go(*cross(g, 1))
        remote(*pass_copy(g, 0, -1)).wait_recv()
        go(*cross(g, -1))
        remote(*pass_copy(g, 0, 2)).wait_recv()
        go(*pass_copy(g, 2, 2))
        go(*pass_copy(g, 2, 1))
        remote(*pass_copy(g, 0, -2)).wait_recv()
        go(*pass_copy(g, -2, -1))
        go(*cross(g, 2))
        go(*cross(g, -2))

    def pass_last(g):
        remote(*pass_copy(g, 2, 1)).wait_recv()
        go(*cross(g, 3))
        remote(*pass_copy(g, -2, -1)).wait_recv()
        go(*cross(g, -3))
        remote(*pass_copy(g, 2, 2)).wait_recv()
        go(*cross(g, 4))
        for off in (0, 1, -1, 2, -2, 3, -3, 4):
            remote(*cross(g, off)).wait_recv()

    def halves(g):
        v = d[g][...].astype(F32)
        return [v[:, :, 8 * k : 8 * k + 8, :HID].reshape(128, HID).astype(BF16) for k in range(2)]

    def x_copy(g, o):
        return (s4.at[g, o - 1], r3.at[g, o - 1], x_send.at[3 * g + o - 1], x_recv.at[3 * g + o - 1], at_x(o))

    def backward(g):
        dg, du = halves(g)
        f = lax.dot_general(dg, bb[:, :HID], NT, preferred_element_type=F32)
        f = adapter_scale * (f + lax.dot_general(du, bb[:, HID:], NT, preferred_element_type=F32))
        e = lax.dot_general(dg, w[0], NT, preferred_element_type=F32)
        e = e + lax.dot_general(du, w[1], NT, preferred_element_type=F32)
        e = e + dot(f.astype(BF16), at[...])
        fac[g] = f
        e6 = e.reshape(2, NX, 2, 8, 1024)
        for rel in range(2):
            cc = oc if rel == 0 else c
            for h in range(2):
                blk = e6[rel, :, h]
                s3[g, :, 2 * h + cc] = jnp.concatenate([blk[:, :, :512], blk[:, :, 512:]], axis=1)
        for o in (2, 1, 3):
            s4[g, o - 1] = s3[g, lax.rem(px + o, NX)].astype(BF16)
            go(*x_copy(g, o))

    def y_copy(g, j):
        to = 2 * j + g
        o = lax.rem(to - py + NY, NY)
        return o, (s5.at[g, j], r5.at[o], y_send.at[g * 4 + j], y_recv.at[o], (row, px * NY + to))

    def x_finish(g):
        total = s3[g, px]
        for o in (1, 3, 2):
            remote(*x_copy(g, o)).wait_recv()
            total = total + r3[g, o - 1].astype(F32)
        s3[g, px] = total
        s5[g] = total.astype(BF16)
        for j in range(4):
            o, copy = y_copy(g, j)

            @pl.when(o != 0)
            def _():
                remote(*copy).start()

    def y_send_wait(g):
        for j in range(4):
            o, copy = y_copy(g, j)

            @pl.when(o != 0)
            def _():
                remote(*copy).wait_send()

    loads[3].wait()
    take(0)
    forward(0)

    for o in range(1, ROWS):
        remote(bblk.at[row], bblk.at[row], b_send.at[o], b_recv.at[o], at_row(o)).wait_recv()
    sum_first(0)
    for r in range(ROWS):
        bf[:, 56 * r : 56 * r + 56] = bblk[r].astype(F32)[:, 0:56]
    bfull = bf[...].astype(BF16)
    bb[...] = jnp.zeros((128, 2 * HID), BF16)
    bb[0:16, 0:HID] = bfull[0:16]
    bb[16:32, HID:] = bfull[16:32]
    at[...] = jnp.zeros((128, 1024), BF16)

    take(1)
    forward(1)

    lane = lax.broadcasted_iota(jnp.int32, (8, 128), 1) // 32

    def regroup(pieces, g):
        out = None
        for q in range(4):
            p = pieces[q]
            shift = (32 * (q - g[q])) % 128
            if shift:
                p = pltpu.roll(p, shift, 1)
            out = p if out is None else jnp.where(lane == q, p, out)
        return out

    v = tblk[:, :, :, :, 512:640].astype(F32).reshape(COLS, 16, 128)
    for tile in range(8):
        four = [v[4 * tile + q, :8] for q in range(4)]
        for j in range(4):
            af[8 * j : 8 * j + 8, 128 * tile : 128 * tile + 128] = regroup(four, (j,) * 4)
    at[0:32, :] = af[...].astype(BF16)
    low_sends()
    sum_first(1)
    sum_second(0)
    sum_second(1)
    loads[4].wait()
    low_half = low_total()
    gate_low = adapter_scale * dot(low_half, bb[:, :HID])
    up_low = adapter_scale * dot(low_half, bb[:, HID:])
    activate(0, gate_low, up_low, low_half)
    activate(1, gate_low, up_low, low_half)
    hid[...] = hidf[...].astype(BF16)
    stores[0].start()
    pass_on(0)
    pass_on(1)
    pass_last(0)
    backward(0)
    pass_last(1)
    backward(1)
    ga = None
    for g in range(2):
        p = dot(fac[g].T[:32].astype(BF16), x[g])
        ga = p if ga is None else ga + p
    for tile in range(8):
        four = [ga[8 * j : 8 * j + 8, 128 * tile : 128 * tile + 128] for j in range(4)]
        for q in range(4):
            yy = 4 * (tile % 2) + q
            ga3[tile // 2, yy // 2, 8 * (yy % 2) : 8 * (yy % 2) + 8, :] = regroup(four, (q,) * 4)

    def ga_x(o):
        return (ga4.at[o - 1], gar.at[o - 1], q_send.at[o - 1], q_recv.at[o - 1], at_x(o))

    for o in (2, 1, 3):
        ga4[o - 1] = ga3[lax.rem(px + o, NX)].astype(BF16)
        go(*ga_x(o))
    x_finish(0)

    low_all = d1[:, :, :, HID:].astype(F32)
    gb = [None, None]
    for g in range(2):
        low_t = low_all[:, :, 8 * g : 8 * g + 8].reshape(128, 128).T[:32].astype(BF16)
        for k, h in enumerate(halves(g)):
            p = dot(low_t, h)[16 * k : 16 * k + 16]
            gb[k] = p if g == 0 else gb[k] + p
    for load in loads[5:]:
        load.wait()
    shift = lax.rem(HID - 56 * row, HID)
    for k in range(2):
        gk = pltpu.roll(adapter_scale * gb[k], shift, 1)[:, :56]
        pb[k], mbo[k], vbo[k] = adam(b[k], mb[k], vb[k], gk)
    for i in (3, 6, 7):
        stores[i].start()
    x_finish(1)
    total = ga3[px]
    for o in (1, 3, 2):
        remote(*ga_x(o)).wait_recv()
        total = total + gar[o - 1].astype(F32)
    ga3[px] = total
    ga5[...] = total.astype(BF16)

    def ga_y(o):
        to = lax.rem(py + o, NY)
        return (ga5.at[to // 2], ga6.at[o], k_send.at[o], k_recv.at[o], (row, px * NY + to))

    for o in FAR_FIRST:
        go(*ga_y(o))
    last = s3[par, px, py // 2]
    for o in (1, 7, 2, 6, 3, 5, 4):
        remote(s5.at[0, 0], r5.at[o], y_send.at[0], y_recv.at[o], at_y(o)).wait_recv()
        last = last + r5[o].astype(F32)
    dxv[:, 0:512] = last[:8].astype(BF16)
    dxv[:, 512:1024] = last[8:].astype(BF16)
    stores[1].start()
    total = ga3[px, py // 2]
    for o in (1, 7, 2, 6, 3, 5, 4):
        remote(*ga_y(o)).wait_recv()
        total = total + ga6[o].astype(F32)
    mine = jnp.where(par == 0, total[:8], total[8:])
    for k in range(2):
        for h in range(2):
            rows = slice(8 * h, 8 * h + 8)
            lanes = 32 * (2 * k + h)
            gk = mine[:, lanes : lanes + 32]
            pa[k, rows, :], mao[k, rows, :], vao[k, rows, :] = adam(
                a[k, rows, :], ma[k, rows, :], va[k, rows, :], gk
            )
    for i in (2, 4, 5):
        stores[i].start()
    for copy in sends:
        copy.wait_send()
    y_send_wait(0)
    y_send_wait(1)
    for store in stores:
        store.wait()


def hand_over(*refs):
    ins, outs, held, (in_sem, out_sem) = refs[:8], refs[8:16], refs[16:24], refs[24:]
    loads = [pltpu.make_async_copy(ins[i], held[i], in_sem.at[i]) for i in range(8)]
    stores = [pltpu.make_async_copy(held[i], outs[i], out_sem.at[i]) for i in range(8)]
    for load in loads:
        load.start()
    for load, store in zip(loads, stores):
        load.wait()
        store.start()
    for store in stores:
        store.wait()


def per_device(tok, cot, w, a, b, ma, va, mb, vb):
    a, ma, va = (jnp.swapaxes(t, 1, 2) for t in (a, ma, va))
    args = (tok, cot, w, a, b, ma, va, mb, vb)
    outs = tuple(jax.ShapeDtypeStruct(t.shape, t.dtype) for t in (cot, tok, a, b, a, a, b, b))
    vmem, dma = pltpu.VMEM, pltpu.SemaphoreType.DMA
    res = pl.pallas_call(
        kernel,
        out_shape=outs,
        in_specs=[pl.BlockSpec(memory_space=pl.ANY)] * 9,
        out_specs=[pl.BlockSpec(memory_space=pl.ANY)] * 8,
        scratch_shapes=[vmem(t.shape, t.dtype) for t in args + outs]
        + [
            vmem((NZ, NC, 2, 16, 640), BF16),
            vmem((8, 128), F32),
            vmem((32, 128), F32),
            vmem((ROWS, 32, 128), BF16),
            vmem((32, HID), F32),
            vmem((128, 2 * HID), BF16),
            vmem((2, 128, 1024), BF16),
            vmem((32, 1024), F32),
            vmem((128, 1024), BF16),
            vmem((2, NZ, 16, HID), F32),
            vmem((2, NZ, 16, HID), BF16),
            vmem((2, NZ, 16, HID), BF16),
            vmem((2, 5, 16, HID), BF16),
            vmem((2, 5, 16, HID), BF16),
            vmem((2, 2, 16, HID), BF16),
            vmem((2, 2, 16, HID), BF16),
            vmem((NC, NZ, 16, 128), BF16),
            vmem((ROWS, 16, 128), BF16),
            vmem((16, HID), F32),
            vmem((NC, NZ, 16, WIDTH[0]), BF16),
            vmem((NC, NZ, 16, WIDTH[1]), BF16),
            vmem((2, 128, 128), F32),
            vmem((2, NX, 4, 16, 512), F32),
            vmem((2, 3, 4, 16, 512), BF16),
            vmem((2, 3, 4, 16, 512), BF16),
            vmem((2, 4, 16, 512), BF16),
            vmem((NY, 16, 512), BF16),
            vmem((NX, 4, 16, 128), F32),
            vmem((3, 4, 16, 128), BF16),
            vmem((3, 4, 16, 128), BF16),
            vmem((4, 16, 128), BF16),
            vmem((NY, 16, 128), BF16),
            dma((9,)), dma((8,)),
            dma((32,)), dma((32,)),
            dma((ROWS,)), dma((ROWS,)),
            dma((2,)), dma((2,)),
            dma((10,)), dma((10,)),
            dma((4,)), dma((4,)),
            dma((ROWS,)), dma((ROWS,)),
            dma((16,)), dma((16,)),
            dma((16,)), dma((16,)),
            dma((6,)), dma((6,)),
            dma((8,)), dma((8,)),
            dma((3,)), dma((3,)),
            dma((8,)), dma((8,)),
        ],
        compiler_params=pltpu.CompilerParams(
            collective_id=0, has_side_effects=True, vmem_limit_bytes=60 * 1024 * 1024
        ),
    )(*args)
    hid, dx, pa, pb, mao, vao, mbo, vbo = pl.pallas_call(
        hand_over,
        out_shape=outs,
        in_specs=[pl.BlockSpec(memory_space=pl.ANY)] * 8,
        out_specs=[pl.BlockSpec(memory_space=pl.ANY)] * 8,
        scratch_shapes=[vmem(t.shape, t.dtype) for t in outs] + [dma((8,)), dma((8,))],
        compiler_params=pltpu.CompilerParams(vmem_limit_bytes=60 * 1024 * 1024),
    )(*res)
    pa, mao, vao = (jnp.swapaxes(t, 1, 2) for t in (pa, mao, vao))
    return hid, dx, pa, pb, mao, vao, mbo, vbo


def solution(mesh):
    placed = (
        P("col", "row"),
        P("row", "col"),
        P(None, "row", "col"),
        P(None, ("row", "col"), None),
        P(None, None, ("col", "row")),
        P(None, ("row", "col"), None),
        P(None, ("row", "col"), None),
        P(None, None, ("col", "row")),
        P(None, None, ("col", "row")),
    )
    return jax.shard_map(
        per_device,
        mesh=mesh,
        in_specs=placed,
        out_specs=(
            P("row", "col"),
            P("col", "row"),
            P(None, ("row", "col"), None),
            P(None, None, ("col", "row")),
            P(None, ("row", "col"), None),
            P(None, ("row", "col"), None),
            P(None, None, ("col", "row")),
            P(None, None, ("col", "row")),
        ),
        check_vma=False,
    )
```

time: 92.1 us -> 67.5 us (0.73)
  local copies, waits for them, and re-layouts: 13.1 us -> 0 us
  Pallas kernels: 77.6 us -> 66.7 us
    pallas_call x1, Pallas kernels: 77.6 us -> 65.1 us  [per_device(): pl.pallas_call(kernel, out_shape=outs, in_specs=[pl.BlockSpec(memory_spac...]
    unnamed x20 -> x0, local copies, waits for them, and re-layouts: 11.1 us -> none
    pallas_call x3 -> x0, local copies, waits for them, and re-layouts: 2.03 us -> none  [per_device(): pl.pallas_call(kernel, out_shape=outs, in_specs=[pl.BlockSpec(memory_spac...]
    pallas_call x0 -> x1, Pallas kernels: none -> 1.58 us  [per_device(): pl.pallas_call(hand_over, out_shape=outs, in_specs=[pl.BlockSpec(memory_s...]
where the time goes in v2:
time: 67.5 us; the launch traced here: 67.3 us
  Pallas kernels  66.7 us (99%)
    pallas_call x1, Pallas kernels, per_device(): pl.pallas_call(kernel, out_shape=outs, in_specs=[pl.BlockSpec(memory_spac...  65.1 us
    pallas_call x1, Pallas kernels, per_device(): pl.pallas_call(hand_over, out_shape=outs, in_specs=[pl.BlockSpec(memory_s...  1.58 us

profile of v2, /device:TPU:1, one launch (start us, length us, event | category | flops | bytes accessed | tf_op | source)
XLA Modules:
  0.0 67.3 jit_solution(404996154417046549)
XLA Ops:
  0.6 65.1 %shard_map.152 = (bf16[16,896]{1,0:T(8,128)(2,1)}, bf16[8,1024]{1,0:T(8,128)(2,1)}, f32[2,16,32]{2,1,0:T(8,128)}, f32[2,16,56]{2,1,0:T(8,128)}, f32[2,16,32]{2,1...) custom-call(bf16[8,1024]{1,0:T(8,128)(2,1)} %tok_h.1, bf16[16,896]{1,0:T(8,128)(2,1)} %cot_h.1, ...), custom_call_target="tpu_custom_call" | custom-call | tf_op jit(solution)/shard_map/pallas_call | solution.py:476
  65.8 1.6 %shard_map.153 = (bf16[16,896]{1,0:T(8,128)(2,1)}, bf16[8,1024]{1,0:T(8,128)(2,1)}, f32[2,16,32]{2,1,0:T(8,128)}, f32[2,16,56]{2,1,0:T(8,128)}, f32[2,16,32]{2,1...) custom-call(bf16[16,896]{1,0:T(8,128)(2,1)} %get-tuple-element.24.refs_0_, ...), custom_call_target="tpu_custom_call" | custom-call | tf_op jit(solution)/shard_map/pallas_call | solution.py:533

commit v3 on v2

--- a/solution.py
+++ b/solution.py
@@ -85,28 +85,34 @@
         copy.start()
         sends.append(copy)
 
+    def settle(most=1000):
+        for copy in sends[:most]:
+            copy.wait_send()
+        del sends[:most]
+
+    barrier = pltpu.get_barrier_semaphore()
+    greet = [at_y(o) for o in FAR_FIRST] + [at_x(o) for o in (2, 1, 3)] + [at_row(o) for o in range(1, ROWS)]
+    for peer in greet:
+        pl.semaphore_signal(barrier, inc=1, device_id=peer, device_id_type=MESH)
+
     loads = [
         pltpu.make_async_copy(h, v, in_sem.at[i])
         for i, (h, v) in enumerate(
             [(tok_h, tok), (a_h, a), (b_h, b), (w_h, w), (cot_h, cot), (ma_h, ma), (va_h, va), (mb_h, mb), (vb_h, vb)]
         )
     ]
-    for load in loads:
+    for load in loads[:3]:
         load.start()
     outs = [(hid, hid_o), (dxv, dx_o), (pa, pa_o), (pb, pb_o), (mao, mao_o), (vao, vao_o), (mbo, mbo_o), (vbo, vbo_o)]
     stores = [pltpu.make_async_copy(v, h, out_sem.at[i]) for i, (v, h) in enumerate(outs)]
 
-    barrier = pltpu.get_barrier_semaphore()
-    greet = (
-        [at_y(o) for o in range(1, NY)] + [at_x(o) for o in range(1, NX)] + [at_row(o) for o in range(1, ROWS)]
-    )
-    for peer in greet:
-        pl.semaphore_signal(barrier, inc=1, device_id=peer, device_id_type=MESH)
+    for load in loads[3:]:
+        load.start()
 
     def block(xx, yy):
         return tblk.at[2 * xx + yy // 4, (yy // 2) % 2, yy % 2]
 
-    for load in loads[:3]:
+    for load in loads[:2]:
         load.wait()
     t = tok[...].astype(F32)
     for k in range(2):
@@ -116,47 +122,79 @@
     own = block(px, py)
     own[:, 0:512] = jnp.concatenate([t[:, :512], t[:, 512:]], axis=0).astype(BF16)
     own[:, 512:640] = jnp.concatenate([aw[...], jnp.zeros((8, 128), F32)], axis=0).astype(BF16)
+    pl.semaphore_wait(barrier, len(greet))
+
+    def blk_at(xo, yy):
+        return block(lax.rem(px - xo + NX, NX), lax.rem(py - yy + NY, NY))
+
+    def t_y(o):
+        return (own, own, t_send.at[o], t_recv.at[o], at_y(o))
+
+    def t_x(yy, xo):
+        blk, i = blk_at(0, yy), 7 + 3 * yy + xo
+        return (blk, blk, t_send.at[i], t_recv.at[i], at_x(xo))
+
+    def t_near(yy, xo):
+        blk, i = blk_at(xo, 0), 7 + 3 * yy + xo
+        return (blk, blk, t_send.at[i], t_recv.at[i], at_y(yy))
+
+    far = [jnp.where(par == 0, e, o) for e, o in zip((2, 6, 4, 3, 5), (3, 5, 2, 6, 4))]
+    for o in far:
+        go(*t_y(o))
+    for o in (2, 1, 3):
+        go(*t_x(0, o))
+    for o in (1, 7):
+        go(*t_y(o))
+    loads[2].wait()
     bw[...] = jnp.zeros((32, 128), F32)
     for k in range(2):
         bw[16 * k : 16 * k + 16, 0:56] = b[k]
-    bblk[row] = bw[...].astype(BF16)
-
-    pl.semaphore_wait(barrier, len(greet))
-
+    bblk[z, c] = bw[...].astype(BF16)
+
+    def b_cross():
+        return (bblk.at[z, c], bblk.at[z, c], b_send.at[0], b_recv.at[0], partner)
+
+    def b_z(o):
+        return (bblk.at[z], bblk.at[z], b_send.at[o], b_recv.at[o], at_z(o))
+
+    go(*b_cross())
+
+    def near(xo):
+        remote(*t_x(0, xo)).wait_recv()
+        go(*t_near(1, xo))
+        go(*t_near(7, xo))
+
+    def spread(i):
+        remote(*t_y(far[i])).wait_recv()
+        for o in (2, 1, 3):
+            go(*t_x(far[i], o))
+
+    near(1)
+    near(3)
+    spread(0)
+    spread(1)
+    near(2)
+    for i in (2, 3, 4):
+        spread(i)
+    remote(*b_cross()).wait_recv()
     for o in FAR_FIRST:
-        go(own, own, t_send.at[o], t_recv.at[o], at_y(o))
-
-    def source(g, j):
-        return lax.rem(jnp.where(par == g, 0, 1) + (0, 2, 6, 4)[j], NY)
-
-    def spread_copy(g, j, o):
-        src = block(px, lax.rem(py - source(g, j) + NY, NY))
-        i = 3 * (4 * g + j) + o - 1
-        return (src, src, t_send.at[8 + i], t_recv.at[8 + i], at_x(o))
-
-    def spread(g, j):
-        off = source(g, j)
-        if j == 0:
-
-            @pl.when(off != 0)
-            def _():
-                remote(own, own, t_send.at[off], t_recv.at[off], at_y(1)).wait_recv()
-        else:
-            remote(own, own, t_send.at[off], t_recv.at[off], at_y(1)).wait_recv()
-        for o in (2, 1, 3):
-            go(*spread_copy(g, j, o))
-
-    for o in range(1, ROWS):
-        go(bblk.at[row], bblk.at[row], b_send.at[o], b_recv.at[o], at_row(o))
-    for j in range(4):
-        spread(0, j)
-    for j in range(4):
-        spread(1, j)
+        go(*b_z(o))
 
     def take(g):
-        for j in range(4):
-            for o in (1, 3, 2):
-                remote(*spread_copy(g, j, o)).wait_recv()
+        @pl.when(par == g)
+        def _():
+            for yy in (2, 6, 4):
+                for o in (1, 3, 2):
+                    remote(*t_x(yy, o)).wait_recv()
+
+        @pl.when(par != g)
+        def _():
+            for yy in (1, 7):
+                remote(*t_y(yy)).wait_recv()
+            for yy in (1, 7, 3, 5):
+                for o in (1, 3, 2):
+                    remote(*t_x(yy, o)).wait_recv()
+
         for rel in range(2):
             u = tblk[:, oc if rel == 0 else c, g].astype(F32)
             x[g, 64 * rel : 64 * rel + 64, 0:512] = u[:, :8, :512].reshape(64, 512).astype(BF16)
@@ -269,6 +307,8 @@
         go(*cross(g, -3))
         remote(*pass_copy(g, 2, 2)).wait_recv()
         go(*cross(g, 4))
+
+    def crossed(g):
         for off in (0, 1, -1, 2, -2, 3, -3, 4):
             remote(*cross(g, off)).wait_recv()
 
@@ -328,11 +368,11 @@
     take(0)
     forward(0)
 
-    for o in range(1, ROWS):
-        remote(bblk.at[row], bblk.at[row], b_send.at[o], b_recv.at[o], at_row(o)).wait_recv()
     sum_first(0)
+    for o in FAR_FIRST:
+        remote(*b_z(o)).wait_recv()
     for r in range(ROWS):
-        bf[:, 56 * r : 56 * r + 56] = bblk[r].astype(F32)[:, 0:56]
+        bf[:, 56 * r : 56 * r + 56] = bblk[r // NC, r % NC].astype(F32)[:, 0:56]
     bfull = bf[...].astype(BF16)
     bb[...] = jnp.zeros((128, 2 * HID), BF16)
     bb[0:16, 0:HID] = bfull[0:16]
@@ -372,11 +412,14 @@
     activate(1, gate_low, up_low, low_half)
     hid[...] = hidf[...].astype(BF16)
     stores[0].start()
+    settle(60)
     pass_on(0)
     pass_on(1)
     pass_last(0)
+    pass_last(1)
+    crossed(0)
     backward(0)
-    pass_last(1)
+    crossed(1)
     backward(1)
     ga = None
     for g in range(2):
@@ -425,6 +468,7 @@
 
     for o in FAR_FIRST:
         go(*ga_y(o))
+    y_send_wait(0)
     last = s3[par, px, py // 2]
     for o in (1, 7, 2, 6, 3, 5, 4):
         remote(s5.at[0, 0], r5.at[o], y_send.at[0], y_recv.at[o], at_y(o)).wait_recv()
@@ -447,9 +491,7 @@
             )
     for i in (2, 4, 5):
         stores[i].start()
-    for copy in sends:
-        copy.wait_send()
-    y_send_wait(0)
+    settle()
     y_send_wait(1)
     for store in stores:
         store.wait()
@@ -483,7 +525,7 @@
             vmem((NZ, NC, 2, 16, 640), BF16),
             vmem((8, 128), F32),
             vmem((32, 128), F32),
-            vmem((ROWS, 32, 128), BF16),
+            vmem((NZ, NC, 32, 128), BF16),
             vmem((32, HID), F32),
             vmem((128, 2 * HID), BF16),
             vmem((2, 128, 1024), BF16),
@@ -514,7 +556,7 @@
             vmem((NY, 16, 128), BF16),
             dma((9,)), dma((8,)),
             dma((32,)), dma((32,)),
-            dma((ROWS,)), dma((ROWS,)),
+            dma((NZ,)), dma((NZ,)),
             dma((2,)), dma((2,)),
             dma((10,)), dma((10,)),
             dma((4,)), dma((4,)),

time: 67.5 us -> 66 us (0.978)
  Pallas kernels: 66.7 us -> 64.9 us
    pallas_call x1, Pallas kernels: 65.1 us -> 63.4 us  [per_device(): pl.pallas_call(kernel, out_shape=outs, in_specs=[pl.BlockSpec(memory_spac...]
where the time goes in v3:
time: 66 us; the launch traced here: 65.6 us
  Pallas kernels  64.9 us (98%)
    pallas_call x1, Pallas kernels, per_device(): pl.pallas_call(kernel, out_shape=outs, in_specs=[pl.BlockSpec(memory_spac...  63.4 us
    pallas_call x1, Pallas kernels, per_device(): pl.pallas_call(hand_over, out_shape=outs, in_specs=[pl.BlockSpec(memory_s...  1.58 us

profile of v3, /device:TPU:1, one launch (start us, length us, event | category | flops | bytes accessed | tf_op | source)
XLA Modules:
  0.0 65.6 jit_solution(1432152251694456639)
XLA Ops:
  0.6 63.4 %shard_map.152 = (bf16[16,896]{1,0:T(8,128)(2,1)}, bf16[8,1024]{1,0:T(8,128)(2,1)}, f32[2,16,32]{2,1,0:T(8,128)}, f32[2,16,56]{2,1,0:T(8,128)}, f32[2,16,32]{2,1...) custom-call(bf16[8,1024]{1,0:T(8,128)(2,1)} %tok_h.1, bf16[16,896]{1,0:T(8,128)(2,1)} %cot_h.1, ...), custom_call_target="tpu_custom_call" | custom-call | tf_op jit(solution)/shard_map/pallas_call | solution.py:518
  64.0 1.6 %shard_map.153 = (bf16[16,896]{1,0:T(8,128)(2,1)}, bf16[8,1024]{1,0:T(8,128)(2,1)}, f32[2,16,32]{2,1,0:T(8,128)}, f32[2,16,56]{2,1,0:T(8,128)}, f32[2,16,32]{2,1...) custom-call(bf16[16,896]{1,0:T(8,128)(2,1)} %get-tuple-element.24.refs_0_, ...), custom_call_target="tpu_custom_call" | custom-call | tf_op jit(solution)/shard_map/pallas_call | solution.py:575

commit v4 on v3

--- a/solution.py
+++ b/solution.py
@@ -338,9 +338,9 @@
             go(*x_copy(g, o))
 
     def y_copy(g, j):
-        to = 2 * j + g
-        o = lax.rem(to - py + NY, NY)
-        return o, (s5.at[g, j], r5.at[o], y_send.at[g * 4 + j], y_recv.at[o], (row, px * NY + to))
+        o = jnp.where(par == g, (4, 2, 6, 0)[j], (3, 5, 1, 7)[j])
+        to = lax.rem(py + o, NY)
+        return o, (s5.at[g, to // 2], r5.at[o], y_send.at[g * 4 + j], y_recv.at[o], (row, px * NY + to))
 
     def x_finish(g):
         total = s3[g, px]
@@ -416,15 +416,13 @@
     pass_on(0)
     pass_on(1)
     pass_last(0)
-    pass_last(1)
     crossed(0)
     backward(0)
+    af[...] = dot(fac[0].T[:32].astype(BF16), x[0])
+    pass_last(1)
     crossed(1)
     backward(1)
-    ga = None
-    for g in range(2):
-        p = dot(fac[g].T[:32].astype(BF16), x[g])
-        ga = p if ga is None else ga + p
+    ga = af[...] + dot(fac[1].T[:32].astype(BF16), x[1])
     for tile in range(8):
         four = [ga[8 * j : 8 * j + 8, 128 * tile : 128 * tile + 128] for j in range(4)]
         for q in range(4):

time: 66 us -> 65.2 us (0.988)
  no operation moved by 1% of the time
where the time goes in v4:
time: 65.2 us; the launch traced here: 65 us
  Pallas kernels  64.3 us (99%)
    pallas_call x1, Pallas kernels, per_device(): pl.pallas_call(kernel, out_shape=outs, in_specs=[pl.BlockSpec(memory_spac...  62.7 us
    pallas_call x1, Pallas kernels, per_device(): pl.pallas_call(hand_over, out_shape=outs, in_specs=[pl.BlockSpec(memory_s...  1.58 us

profile of v4, /device:TPU:1, one launch (start us, length us, event | category | flops | bytes accessed | tf_op | source)
XLA Modules:
  0.0 65.0 jit_solution(859684662206279213)
XLA Ops:
  0.6 62.7 %shard_map.152 = (bf16[16,896]{1,0:T(8,128)(2,1)}, bf16[8,1024]{1,0:T(8,128)(2,1)}, f32[2,16,32]{2,1,0:T(8,128)}, f32[2,16,56]{2,1,0:T(8,128)}, f32[2,16,32]{2,1...) custom-call(bf16[8,1024]{1,0:T(8,128)(2,1)} %tok_h.1, bf16[16,896]{1,0:T(8,128)(2,1)} %cot_h.1, ...), custom_call_target="tpu_custom_call" | custom-call | tf_op jit(solution)/shard_map/pallas_call | solution.py:516
  63.4 1.6 %shard_map.153 = (bf16[16,896]{1,0:T(8,128)(2,1)}, bf16[8,1024]{1,0:T(8,128)(2,1)}, f32[2,16,32]{2,1,0:T(8,128)}, f32[2,16,56]{2,1,0:T(8,128)}, f32[2,16,32]{2,1...) custom-call(bf16[16,896]{1,0:T(8,128)(2,1)} %get-tuple-element.24.refs_0_, ...), custom_call_target="tpu_custom_call" | custom-call | tf_op jit(solution)/shard_map/pallas_call | solution.py:573

commit v5 on v4

--- a/solution.py
+++ b/solution.py
@@ -68,9 +68,6 @@
     def at_x(off):
         return (row, lax.rem(px + off, NX) * NY + py)
 
-    def at_row(off):
-        return (lax.rem(row + off, ROWS), col)
-
     partner = (z * NC + oc, col)
 
     def remote(src, dst, send, recv, to):
@@ -91,7 +88,7 @@
         del sends[:most]
 
     barrier = pltpu.get_barrier_semaphore()
-    greet = [at_y(o) for o in FAR_FIRST] + [at_x(o) for o in (2, 1, 3)] + [at_row(o) for o in range(1, ROWS)]
+    greet = [at_y(o) for o in FAR_FIRST] + [at_x(o) for o in (2, 1, 3)] + [at_z(o) for o in FAR_FIRST] + [partner]
     for peer in greet:
         pl.semaphore_signal(barrier, inc=1, device_id=peer, device_id_type=MESH)
 
@@ -236,24 +233,31 @@
         sb[g, 1] = (yo[g, zc(-2)] + ra[g, 2].astype(F32)).astype(BF16)
         go(*second_copy(g, 1))
 
-    def low_copy(o):
-        to = lax.rem(row + o, ROWS)
-        rel = jnp.where(to % NC == c, 1, 0)
-        return (lows.at[rel, to // NC], lowr.at[o], l_send.at[o], l_recv.at[o], (to, col))
+    def low_cross():
+        return (lows.at[0], lowr.at[0], l_send.at[0], l_recv.at[0], partner)
+
+    def low_z(o):
+        to = lax.rem(z + o, NZ)
+        return (lows.at[1, to], lowr.at[1, o], l_send.at[o], l_recv.at[o], (to * NC + c, col))
 
     def low_sends():
         both = [
             lax.dot_general(x[g], at[...], NT, preferred_element_type=F32).reshape(NC, NZ, 8, 128) for g in range(2)
         ]
         lows[...] = jnp.concatenate(both, axis=2).astype(BF16)
-        for o in range(1, ROWS):
-            go(*low_copy(o))
+        go(*low_cross())
+
+    def low_next():
+        remote(*low_cross()).wait_recv()
+        lows[1] = (lows[1].astype(F32) + lowr[0].astype(F32)).astype(BF16)
+        for o in FAR_FIRST:
+            go(*low_z(o))
 
     def low_total():
         total = lows[1, z].astype(F32)
-        for o in range(1, ROWS):
-            remote(*low_copy(o)).wait_recv()
-            total = total + lowr[o].astype(F32)
+        for o in FAR_FIRST:
+            remote(*low_z(o)).wait_recv()
+            total = total + lowr[1, o].astype(F32)
         keep = lax.broadcasted_iota(jnp.int32, (16, 128), 1) < 32
         return jnp.where(keep, total, 0.0).astype(BF16)
 
@@ -402,6 +406,7 @@
     at[0:32, :] = af[...].astype(BF16)
     low_sends()
     sum_first(1)
+    low_next()
     sum_second(0)
     sum_second(1)
     loads[4].wait()
@@ -537,7 +542,7 @@
             vmem((2, 2, 16, HID), BF16),
             vmem((2, 2, 16, HID), BF16),
             vmem((NC, NZ, 16, 128), BF16),
-            vmem((ROWS, 16, 128), BF16),
+            vmem((NC, NZ, 16, 128), BF16),
             vmem((16, HID), F32),
             vmem((NC, NZ, 16, WIDTH[0]), BF16),
             vmem((NC, NZ, 16, WIDTH[1]), BF16),

time: 65.2 us -> 65.5 us (level)
  no operation moved by 1% of the time
where the time goes in v5:
time: 65.5 us; the launch traced here: 65 us
  Pallas kernels  64.4 us (98%)
    pallas_call x1, Pallas kernels, per_device(): pl.pallas_call(kernel, out_shape=outs, in_specs=[pl.BlockSpec(memory_spac...  62.8 us
    pallas_call x1, Pallas kernels, per_device(): pl.pallas_call(hand_over, out_shape=outs, in_specs=[pl.BlockSpec(memory_s...  1.58 us

profile of v5, /device:TPU:1, one launch (start us, length us, event | category | flops | bytes accessed | tf_op | source)
XLA Modules:
  0.0 65.0 jit_solution(1282834089490274526)
XLA Ops:
  0.6 62.8 %shard_map.152 = (bf16[16,896]{1,0:T(8,128)(2,1)}, bf16[8,1024]{1,0:T(8,128)(2,1)}, f32[2,16,32]{2,1,0:T(8,128)}, f32[2,16,56]{2,1,0:T(8,128)}, f32[2,16,32]{2,1...) custom-call(bf16[8,1024]{1,0:T(8,128)(2,1)} %tok_h.1, bf16[16,896]{1,0:T(8,128)(2,1)} %cot_h.1, ...), custom_call_target="tpu_custom_call" | custom-call | tf_op jit(solution)/shard_map/pallas_call | solution.py:521
  63.4 1.6 %shard_map.153 = (bf16[16,896]{1,0:T(8,128)(2,1)}, bf16[8,1024]{1,0:T(8,128)(2,1)}, f32[2,16,32]{2,1,0:T(8,128)}, f32[2,16,56]{2,1,0:T(8,128)}, f32[2,16,32]{2,1...) custom-call(bf16[16,896]{1,0:T(8,128)(2,1)} %get-tuple-element.24.refs_0_, ...), custom_call_target="tpu_custom_call" | custom-call | tf_op jit(solution)/shard_map/pallas_call | solution.py:578
